TPU v7x, 128 devices: a whole 4x4x4 slice. The times are simulated.
128 devices in a mesh: seq: 16 (over z, x_hi, core), ctx: 8 (over y, x_lo).
Axes of the slice: x: 4 (x_hi: 2, x_lo: 2; x = x_hi * 2 + x_lo), y: 4, z: 4, core: 2. Of those that a mesh axis runs over, the one named last changes fastest.
Arguments:
- tokens: bfloat16 [16, 1024, 1024], P('seq', 'ctx'), may hold values from -6 to 6
- cotangent: bfloat16 [16, 1024, 1024], P('seq', 'ctx'), may hold values from -6 to 6
- segments: int32 [16, 1024], P('seq'), may hold values from 0 to 47, as said below
- positions: int32 [16, 1024], P('seq', 'ctx'), may hold values from 0 to 1021, as said below
- attention_gain: bfloat16 [1024], P(('seq', 'ctx')), may hold values from 0.25 to 1.75
- projection: bfloat16 [1024, 4096], P(('seq', 'ctx')), may hold values from -0.1875 to 0.1875
- head_gain: bfloat16 [256], P(('seq', 'ctx')), may hold values from 0.25 to 1.75
- output_weight: bfloat16 [2048, 1024], P(('seq', 'ctx')), may hold values from -0.75 to 0.75
- feed_gain: bfloat16 [1024], P(('seq', 'ctx')), may hold values from 0.25 to 1.75
- expansion: bfloat16 [1024, 6144], P(('seq', 'ctx')), may hold values from -0.1875 to 0.1875
- contraction: bfloat16 [3072, 1024], P(('seq', 'ctx')), may hold values from -0.21875 to 0.21875
Outputs:
- layer_out: bfloat16 [16, 1024, 1024], P('seq', 'ctx')
- grad_tokens: float32 [16, 1024, 1024], P('seq', 'ctx')
- grad_attention_gain: float32 [1024], P(('seq', 'ctx'))
- grad_projection: float32 [1024, 4096], P(('seq', 'ctx'))
- grad_head_gain: float32 [256], P(('seq', 'ctx'))
- grad_output_weight: float32 [2048, 1024], P(('seq', 'ctx'))
- grad_feed_gain: float32 [1024], P(('seq', 'ctx'))
- grad_expansion: float32 [1024, 6144], P(('seq', 'ctx'))
- grad_contraction: float32 [3072, 1024], P(('seq', 'ctx'))
Inputs may be any that keep to these rules, and one draw needn't show every extreme that they name: `segments`: along each sequence the ids never fall; sequence s holds the documents 3 s, 3 s + 1 and 3 s + 2; the first and the last of them hold 1 to 127 tokens each, the middle one the rest. `positions`: a token's index within its document, 0 at the document's first token.
All inputs are finite; a program needn't handle non-finite values.
Results may differ from a plain program's by a relative error of at most 0.03.
Values may be sent and summed in bfloat16 or wider, within the bound.
A program may use at most 192 MiB of HBM per device.

v0:
```python
import math

import jax
import jax.numpy as jnp
from jax import lax
from jax.experimental import pallas as pl
from jax.experimental.pallas import tpu as pltpu
from jax.sharding import PartitionSpec as P

F32 = jnp.float32
BF16 = jnp.bfloat16
MESH = pl.DeviceIdType.MESH
EPS = 1e-06
THETA = 1000000.0
NEGATIVE = -1e30
D = 1024
HEAD = 128
FF = 3072
FL = 768
TOK = 128
SEQ = 1024
QB = 256
SCALE = HEAD**-0.5


def dot(a, b, da=1, db=0):
    return lax.dot_general(a, b, (((da,), (db,)), ((), ())), preferred_element_type=F32)


def rows(start, size):
    return pl.ds(pl.multiple_of(start, size), size)


SCRATCH = dict(
    pa=((8, 8, D), BF16),
    pw=((8, 2, 64, D), BF16),
    ea=((8, 8, 1536), BF16),
    ew=((4, 2, 2, 64, 1536), BF16),
    ow=((2, 2, 4, 2, 16, D), BF16),
    cb=((2, 2, 4, 2, 24, D), BF16),
    cw=((FL, D), BF16),
    gi=((24, 128), F32),
    ga=((8, 24, 128), F32),
    gb=((8, 24, 128), F32),
    gsum=((24, 128), F32),
    gacc=((24, 128), F32),
    gfr=((24, 128), F32),
    gall=((24, 128), F32),
    cos=((512, HEAD), F32),
    sin=((512, HEAD), F32),
    segc=((QB, 128), jnp.int32),
    xs=((512, D), BF16),
    ns=((512, D), BF16),
    pj=((512, 768), F32),
    qs=((2, 4, QB, HEAD), BF16),
    kv=((8, 4, TOK, HEAD), BF16),
    mx=((512, 512), BF16),
    ps=((4, TOK, D), BF16),
    r1=((4, TOK, D), BF16),
    hid=((TOK, D), F32),
    nm=((512, D), BF16),
    dy=((512, D), BF16),
    act=((512, FL), BF16),
    ggu=((512, 1536), BF16),
    gs=((4, TOK, D), BF16),
    r2=((4, TOK, D), BF16),
    los=((4, TOK, D), BF16),
    r3=((4, TOK, D), BF16),
    gh=((TOK, D), F32),
    g4=((512, D), BF16),
    gm=((2, 4, QB, HEAD), BF16),
    f4=((4096, HEAD), F32),
    dq=((2, 4, QB, HEAD), F32),
    ds=((2, 4, 2, TOK, HEAD), BF16),
    dr=((2, 4, 2, TOK, HEAD), BF16),
    gp=((512, D), BF16),
    attg=((1, D), F32),
    hgq=((1, HEAD), F32),
    hgk=((1, HEAD), F32),
    gg0=((24, 128), F32),
    gg1=((24, 128), F32),
    ggt=((24, 128), F32),
    ggt2=((24, 128), F32),
    gg2=((8, 24, 128), F32),
    gg3=((8, 24, 128), F32),
    ge=((2, 8, 64, 1536), BF16),
    ge1=((8, 64, 1536), BF16),
    ges=((8, 64, 1536), BF16),
    ge2=((4, 2, 64, 1536), BF16),
    get=((2, 64, 1536), BF16),
    gex=((64, 1536), BF16),
    gef=((8, 8, 1536), BF16),
    ge3=((8, 8, 1536), BF16),
    gc=((2, 2, 8, 24, D), BF16),
    gc1=((2, 8, 24, D), BF16),
    gcs=((2, 2, 4, 24, D), BF16),
    gc2=((4, 4, 24, D), BF16),
    gcf=((4, 24, D), BF16),
    gc3=((4, 24, D), BF16),
    go=((2, 2, 8, 16, D), BF16),
    go1=((2, 8, 16, D), BF16),
    gos=((2, 2, 4, 16, D), BF16),
    go2=((4, 4, 16, D), BF16),
    gof=((4, 16, D), BF16),
    go3=((4, 16, D), BF16),
    gpx=((1536, D), BF16),
    gp1=((512, D), BF16),
    gp2=((8, 64, D), BF16),
    gpf=((8, 8, D), BF16),
    gp3=((8, 8, D), BF16),
)
RECV = dict(
    pa=(8, 2), ea=8, ga=8, gb=8, gfr=1, x=4, dy=4, pb=(2, 8), eb=(2, 4), ps=2, es=2,
    o1=4, o2=4, o3=2, c1=4, c2=4, c3=2, kv=4, r1=4, nm=4, r2=4, r3=4, g4=4, dr=(2, 4), r4=4,
    e1=1, e2=4, ex=1, e3=8, c4=2, c5=4, c6=4, o4=2, o5=4, o6=4, p1=2, p2=(2, 8), p3=8, a1=1, a2=8, a3=8,
)
N_SEND = 160
NAMES = (
    ["x", "dyi", "pi", "oi", "ei", "ci", "agi", "fgi", "hgi", "segr"]
    + ["lo", "gt", "gpo", "goo", "geo", "gco", "ggo"]
    + list(SCRATCH)
    + ["s_" + n for n in RECV]
    + ["send", "loc"]
)
PLACES = (
    (0, (0, 256)), (256, (512, 128)), (384, (768, 128)),
    (512, (256, 256)), (768, (640, 128)), (896, (896, 128)),
)
HEADS = (0, 128, 256, 384, 512, 768)
PCOLS = ((0, 512, 0), (2048, 256, 512), (3072, 256, 768))


class Box:
    pass


def kernel(*refs):
    r = Box()
    for name, ref in zip(NAMES, refs, strict=True):
        setattr(r, name, ref)
    s, c = lax.axis_index("seq"), lax.axis_index("ctx")
    z, xh, core = s // 4, (s // 2) % 2, s % 2
    y, xl = c // 2, c % 2
    w = s // 2
    sib = 1 - core

    def at(zz, xx, cc, ctx):
        return {"seq": zz * 4 + xx * 2 + cc, "ctx": ctx}

    def on_w(ww, cc, ctx):
        return {"seq": ww * 2 + cc, "ctx": ctx}

    me_sib = on_w(w, sib, c)
    ctx_peer = [None] + [lax.rem(c + k, 8) for k in range(1, 8)]
    ctx_from = [None] + [lax.rem(c + 8 - k, 8) for k in range(1, 8)]
    w_peer = [None] + [lax.rem(w + k, 8) for k in range(1, 8)]
    w_from = [None] + [lax.rem(w + 8 - k, 8) for k in range(1, 8)]
    y_peer = [None] + [lax.rem(y + k, 4) for k in range(1, 4)]
    y_from = [None] + [lax.rem(y + 4 - k, 4) for k in range(1, 4)]
    z_peer = [None] + [lax.rem(z + k, 4) for k in range(1, 4)]
    z_from = [None] + [lax.rem(z + 4 - k, 4) for k in range(1, 4)]
    x_line = [(xh, 1 - xl), (1 - xh, xl), (1 - xh, 1 - xl)]
    diag = y == z

    def e_block(zz, xx, cc):
        return r.ew.at[zz, xx, cc]

    def all_p(start, stop):
        return r.pw[:, :, :, start:stop].reshape(D, stop - start)

    def all_e():
        return r.ew[...].reshape(D, 1536)

    def all_o():
        return r.ow[...].reshape(512, D)

    free, sends = list(range(N_SEND - 1)), []

    def send(src, dst, sem, dev, unless=None):
        at = free.pop(0)
        cp = pltpu.make_async_remote_copy(
            src_ref=src, dst_ref=dst, send_sem=r.send.at[at], recv_sem=sem,
            device_id=dev, device_id_type=MESH,
        )
        sends.append((cp, unless, at))
        if unless is None:
            cp.start()
        else:
            pl.when(jnp.logical_not(unless))(cp.start)

    def finish(some):
        for entry in some:
            cp, unless, at = entry
            if unless is None:
                cp.wait_send()
            else:
                pl.when(jnp.logical_not(unless))(cp.wait_send)
            free.append(at)
        sends[:] = [e for e in sends if not any(e is f for f in some)]

    def got(dst, sem):
        pltpu.make_async_remote_copy(
            src_ref=dst, dst_ref=dst, send_sem=r.send.at[N_SEND - 1], recv_sem=sem,
            device_id=me_sib, device_id_type=MESH,
        ).wait_recv()

    bar = pltpu.get_barrier_semaphore()

    def greet(dev):
        pl.semaphore_signal(bar, inc=1, device_id=dev, device_id_type=MESH)

    greet(me_sib)
    for k in range(1, 8):
        greet({"seq": s, "ctx": ctx_peer[k]})
        greet(on_w(w_peer[k], core, c))
    greet(at(z, x_line[2][0], core, 2 * y + x_line[2][1]))
    for zz in range(4):

        @pl.when(jnp.logical_not(diag & (z == zz)))
        def _():
            greet(at(zz, xh, core, 2 * z + xl))
            greet(at(y, xh, core, 2 * zz + xl))

    own = []

    def own_copy(src, dst):
        cp = pltpu.make_async_copy(src, dst, r.loc.at[len(own)])
        own.append(cp)
        cp.start()

    my4 = rows(y * TOK, TOK)
    own_copy(r.x, r.xs.at[my4])
    own_copy(r.dyi, r.dy.at[my4])
    for start, size, place in PCOLS:
        own_copy(
            r.pi.at[:, pl.ds(pl.multiple_of(start + y * size, size), size)],
            r.pa.at[c, :, pl.ds(place, size)],
        )
    for part in range(2):
        own_copy(
            r.ei.at[:, pl.ds(pl.multiple_of(part * FF + y * FL, FL), FL)],
            r.ea.at[c, :, pl.ds(part * FL, FL)],
        )

    tile_row = lax.broadcasted_iota(jnp.int32, (8, 128), 0)
    tile_lane = lax.broadcasted_iota(jnp.int32, (8, 128), 1)
    flat = tile_row * 128 + tile_lane
    place = 8 * s + c
    for n, (ref, size) in enumerate(((r.agi, 8), (r.fgi, 8), (r.hgi, 2))):
        values = ref[...].astype(F32)
        tile = jnp.zeros((8, 128), F32)
        for j in range(size):
            tile = jnp.where(flat == place * size + j, values[:, j : j + 1], tile)
        r.gi[8 * n : 8 * n + 8, :] = tile

    pl.semaphore_wait(bar, 24 - jnp.where(diag, 2, 0))

    for k in range(1, 8):
        send(r.gi, r.ga.at[c], r.s_ga.at[k], {"seq": s, "ctx": ctx_peer[k]})
    for part in (1, 2, 0):
        start, size, place = PCOLS[part]
        for k in range(1, 8):
            to = ctx_peer[k]
            send(
                r.pi.at[:, pl.ds(pl.multiple_of(start + (to // 2) * size, size), size)],
                r.pa.at[c, :, pl.ds(place, size)],
                r.s_pa.at[k, min(part, 1)],
                {"seq": s, "ctx": to},
            )
    for k in (1, 3, 2):
        send(r.x, r.xs.at[my4], r.s_x.at[k], {"seq": s, "ctx": 2 * y_peer[k] + xl})

    @pl.when(diag)
    def _():
        a = pltpu.make_async_copy(
            r.oi,
            r.ow.at[xh, core, y, xl],
            r.loc.at[14],
        )
        b = pltpu.make_async_copy(r.ci, r.cb.at[xh, core, y, xl], r.loc.at[15])
        a.start()
        b.start()
        a.wait()
        b.wait()

    for cp in own:
        cp.wait()

    lane = lax.broadcasted_iota(jnp.int32, (1, HEAD), 1)
    index = jnp.where(lane < HEAD // 2, lane, lane - HEAD // 2).astype(F32)
    inverse = jnp.exp(index * (-2.0 / HEAD * math.log(THETA)))
    sign = jnp.where(lane < HEAD // 2, -1.0, 1.0)
    eye = lax.broadcasted_iota(jnp.int32, (TOK, TOK), 0) == lax.broadcasted_iota(
        jnp.int32, (TOK, TOK), 1
    )
    for j in range(4):
        b = pl.ds(j * TOK, TOK)
        seg = r.segr[:, pl.ds(pl.multiple_of((2 * j + xl) * TOK, TOK), TOK)]
        seg = jnp.sum(jnp.where(eye, seg.astype(F32), 0.0), axis=1, keepdims=True)
        r.segc[:, j : j + 1] = jnp.concatenate([seg, seg], 0).astype(jnp.int32)
        before = jnp.sum((r.segr[...].astype(F32) < seg).astype(F32), axis=1, keepdims=True)
        t = lax.broadcasted_iota(jnp.int32, (TOK, 1), 0) + (2 * j + xl) * TOK
        phase = (t.astype(F32) - before) * inverse
        r.cos[b, :] = jnp.cos(phase)
        r.sin[b, :] = jnp.sin(phase) * sign

    kv_half, q_half = pl.ds(512, 512), pl.ds(0, 512)

    def spread(n, half):
        blk = r.pw.at[w, core, :, half]
        for k in range(1, 8):
            send(blk, blk, r.s_pb.at[n, k], on_w(w_peer[k], core, c))

    def pass_on(n, half):
        for k in range(1, 8):
            got(r.pw.at[w_from[k], core, :, half], r.s_pb.at[n, k])
        blk = r.pw.at[:, core, :, half]
        send(blk, blk, r.s_ps.at[n], me_sib)

    def from_sibling(n, half):
        got(r.pw.at[:, sib, :, half], r.s_ps.at[n])

    def joined(start, size):
        return jnp.concatenate(
            [r.pa[j, :, start : start + size].astype(F32) for j in range(8)], 0
        ).astype(BF16)

    total = r.gi[...]
    for k in range(1, 8):
        got(r.ga.at[ctx_from[k]], r.s_ga.at[k])
        total = total + r.ga[ctx_from[k]]
    r.gsum[...] = total
    for k in range(1, 8):
        send(r.gsum, r.gb.at[w], r.s_gb.at[k], on_w(w_peer[k], core, c))
    for k in range(1, 8):
        got(r.pa.at[ctx_from[k], :, kv_half], r.s_pa.at[k, 1])
    for g in range(2):
        r.pw[w, core, :, 512 + g * 256 : 640 + g * 256] = joined(512 + g * 128, 128)
        r.pw[w, core, :, 640 + g * 256 : 768 + g * 256] = joined(768 + g * 128, 128)
    spread(0, kv_half)
    for k in range(1, 8):
        to = ctx_peer[k]
        for part in range(2):
            send(
                r.ei.at[:, pl.ds(pl.multiple_of(part * FF + (to // 2) * FL, FL), FL)],
                r.ea.at[c, :, pl.ds(part * FL, FL)],
                r.s_ea.at[k],
                {"seq": s, "ctx": to},
            )
    for k in range(1, 8):
        got(r.pa.at[ctx_from[k], :, q_half], r.s_pa.at[k, 0])
    r.pw[w, core, :, 0:512] = joined(0, 512)
    total = r.gsum[...]
    for k in range(1, 8):
        got(r.gb.at[w_from[k]], r.s_gb.at[k])
        total = total + r.gb[w_from[k]]
    r.gacc[...] = total
    send(r.gacc, r.gfr, r.s_gfr.at[0], me_sib)
    for zz in range(4):
        send(
            r.oi,
            r.ow.at[xh, core, y, xl],
            r.s_o1.at[y],
            at(zz, xh, core, 2 * z + xl),
            unless=diag & (z == zz),
        )
    pass_on(0, kv_half)
    spread(1, q_half)
    got(r.gfr, r.s_gfr.at[0])
    r.gall[...] = r.gacc[...] + r.gfr[...]
    from_sibling(0, kv_half)

    def wide(first):
        return jnp.concatenate([r.gall[first + j : first + j + 1, :] for j in range(8)], 1)

    gain_a, gain_f = wide(0), wide(8)
    gain_q, gain_k = r.gall[16:17, :], r.gall[17:18, :]

    def turn(v):
        return pltpu.roll(v, HEAD // 2, 1)

    x_partner = {"seq": s, "ctx": 2 * y + 1 - xl}
    def headed(u, b, h):
        r.pj[b, h * HEAD : (h + 1) * HEAD] = u
        ui = lax.rsqrt(jnp.mean(u * u, axis=1, keepdims=True) + EPS)
        u = u * ui * (gain_q if h < 4 else gain_k)
        return (u * r.cos[b, :] + turn(u) * r.sin[b, :]).astype(BF16)

    for k in (0, 1, 3, 2):
        j = y if k == 0 else y_from[k]
        b = rows(j * TOK, TOK)
        if k:
            got(r.xs.at[b], r.s_x.at[k])
        v = r.xs[b, :].astype(F32)
        inv = lax.rsqrt(jnp.mean(v * v, axis=1, keepdims=True) + EPS)
        n = (v * inv * gain_a).astype(BF16)
        r.ns[b, :] = n
        out = dot(n, all_p(512, D))
        mine = 2 * j + xl
        for g in range(2):
            r.kv[mine, g] = headed(out[:, g * 256 : g * 256 + HEAD], b, 4 + g)
            r.kv[mine, 2 + g] = out[:, g * 256 + HEAD : g * 256 + 256].astype(BF16)
        send(r.kv.at[mine], r.kv.at[mine], r.s_kv.at[j], x_partner)

    for k in (1, 3, 2):
        send(r.dyi, r.dy.at[my4], r.s_dy.at[k], {"seq": s, "ctx": 2 * y_peer[k] + xl})

    for k in range(1, 8):
        got(r.ea.at[ctx_from[k]], r.s_ea.at[k])
    r.ew[z, xh, core] = jnp.concatenate([r.ea[j].astype(F32) for j in range(8)], 0).astype(BF16)
    own_e = r.ew.at[z, xh, core]
    for k in (1, 3, 2):
        send(own_e, own_e, r.s_eb.at[0, k], at(z_peer[k], xh, core, c))
    for zz in range(4):
        send(
            r.ci,
            r.cb.at[xh, core, y, xl],
            r.s_c1.at[y],
            at(zz, xh, core, 2 * z + xl),
            unless=diag & (z == zz),
        )

    pass_on(1, q_half)
    from_sibling(1, q_half)
    for j in range(4):
        b = pl.ds(j * TOK, TOK)
        out = dot(r.ns[b, :], all_p(0, 512))
        for h in range(4):
            u = headed(out[:, h * HEAD : (h + 1) * HEAD], b, h)
            r.qs[h // 2, j, pl.ds((h % 2) * TOK, TOK), :] = u
    for j in range(4):

        @pl.when(jnp.logical_not(diag & (y == j)))
        def _():
            got(r.ow.at[xh, core, j, xl], r.s_o1.at[j])

    blk = r.ow.at[xh, core, :, xl]
    for n, (xx, ll) in enumerate(x_line):
        send(blk, blk, r.s_o2.at[n], at(z, xx, core, 2 * y + ll))
    send(own_e, own_e, r.s_eb.at[0, 0], at(z, 1 - xh, core, c))


    def mask(j):
        n = (2 * j + 2) * TOK
        row = lax.broadcasted_iota(jnp.int32, (QB, n), 0)
        t = (2 * j + xl) * TOK + jnp.where(row < TOK, row, row - TOK)
        u = lax.broadcasted_iota(jnp.int32, (QB, n), 1)
        return (u <= t) & (r.segr[:, :n] == r.segc[:, j : j + 1])

    def at_p(g, j):
        n = (2 * j + 2) * TOK
        if j == 1:
            return r.gpx.at[D : D + QB, g * n : (g + 1) * n]
        first = g * QB + (0 if j == 3 else 2 * QB)
        return r.gpx.at[first : first + QB, 0:n] if j else r.gpx.at[first : first + QB, D - n : D]

    def keys(h, j):
        n = 2 * j + 2
        return r.kv[:n, h].reshape(n * TOK, HEAD)

    for j in range(4):
        got(r.kv.at[2 * j + 1 - xl], r.s_kv.at[j])
        ok = mask(j)
        b = pl.ds(j * TOK, TOK)
        for g in range(2):
            sc = dot(r.qs[g, j], keys(g, j), 1, 1) * SCALE
            sc = jnp.where(ok, sc, NEGATIVE)
            top = jnp.max(sc, axis=1, keepdims=True)
            e = jnp.exp(sc - top)
            tot = jnp.sum(e, axis=1, keepdims=True)
            p = (e * (1.0 / tot)).astype(BF16)
            at_p(g, j)[...] = p
            o = dot(p, keys(2 + g, j)).astype(BF16)
            r.mx[b, (2 * g) * HEAD : (2 * g + 1) * HEAD] = o[:TOK, :]
            r.mx[b, (2 * g + 1) * HEAD : (2 * g + 2) * HEAD] = o[TOK:, :]
        if j == 2:
            for n, (xx, ll) in enumerate(x_line):
                got(r.ow.at[xx, core, :, ll], r.s_o2.at[n])
            for n in range(2):
                send(r.ow.at[n, core], r.ow.at[n, core], r.s_o3.at[n], me_sib)
    for n in range(2):
        got(r.ow.at[n, sib], r.s_o3.at[n])
    for k in (2, 1, 3, 0):
        j = y_peer[k] if k else y
        r.ps[j] = dot(r.mx[rows(j * TOK, TOK), :], all_o()).astype(BF16)
        if k:
            send(r.ps.at[j], r.r1.at[y], r.s_r1.at[y], {"seq": s, "ctx": 2 * j + xl})

    blk = e_block(z, 1 - xh, core)
    got(blk, r.s_eb.at[0, 0])
    for k in (1, 3, 2):
        send(blk, blk, r.s_eb.at[1, k], at(z_peer[k], xh, core, c))
    for k in (1, 3, 2):
        got(e_block(z_from[k], xh, core), r.s_eb.at[0, k])
    blk = r.ew.at[:, xh, core]
    send(blk, blk, r.s_es.at[0], me_sib)
    for j in range(4):

        @pl.when(jnp.logical_not(diag & (y == j)))
        def _():
            got(r.cb.at[xh, core, j, xl], r.s_c1.at[j])

    blk = r.cb.at[xh, core, :, xl]
    for n, (xx, ll) in enumerate(x_line):
        send(blk, blk, r.s_c2.at[n], at(z, xx, core, 2 * y + ll))

    hidden = r.xs[my4, :].astype(F32) + r.ps[y].astype(F32)
    for k in range(1, 4):
        got(r.r1.at[y_from[k]], r.s_r1.at[y_from[k]])
        hidden = hidden + r.r1[y_from[k]].astype(F32)
    r.hid[...] = hidden
    inv_h = lax.rsqrt(jnp.mean(hidden * hidden, axis=1, keepdims=True) + EPS)
    r.nm[my4, :] = (hidden * inv_h * gain_f).astype(BF16)
    def send_nm(k):
        send(
            r.nm.at[my4], r.nm.at[my4], r.s_nm.at[k], {"seq": s, "ctx": 2 * y_peer[k] + xl}
        )

    older = list(sends)
    send_nm(1)
    send_nm(3)
    for k in (1, 3, 2):
        got(e_block(z_from[k], 1 - xh, core), r.s_eb.at[1, k])
    blk = r.ew.at[:, 1 - xh, core]
    send(blk, blk, r.s_es.at[1], me_sib)

    for n, (xx, ll) in enumerate(x_line):
        got(r.cb.at[xx, core, :, ll], r.s_c2.at[n])
    for n in range(2):
        send(r.cb.at[n, core], r.cb.at[n, core], r.s_c3.at[n], me_sib)
    for k in range(1, 4):
        got(r.dy.at[rows(y_from[k] * TOK, TOK)], r.s_dy.at[k])
    finish(older)
    for n in range(2):
        got(r.cb.at[n, sib], r.s_c3.at[n])
    got(r.ew.at[:, xh, sib], r.s_es.at[0])
    got(r.ew.at[:, 1 - xh, sib], r.s_es.at[1])
    for j in range(16):
        r.cw[48 * j : 48 * j + 48, :] = jnp.concatenate(
            [r.cb[j // 8, j // 4 % 2, j % 4, n].astype(F32) for n in range(2)], 0
        ).astype(BF16)

    def grad_act(k, _):
        b = rows(k * TOK, TOK)
        g = dot(r.dy[b, :], r.cw[...], 1, 1)
        for h in range(6):
            r.f4[rows(h * 512 + k * TOK, TOK), :] = g[:, h * HEAD : (h + 1) * HEAD]
        return 0

    lax.fori_loop(0, 4, grad_act, 0)

    for k in (0, 1, 3, 2):
        b4 = y if k == 0 else y_from[k]
        b = rows(b4 * TOK, TOK)
        if k:
            got(r.nm.at[b], r.s_nm.at[k])
        gu = dot(r.nm[b, :], all_e())
        gate, up = gu[:, :FL], gu[:, FL:]
        sg = 1.0 / (1.0 + jnp.exp(-gate))
        sl = gate * sg
        r.act[b, :] = (sl * up).astype(BF16)
        gt = jnp.concatenate([r.f4[rows(h * 512 + b4 * TOK, TOK), :] for h in range(6)], 1)
        r.ggu[b, :FL] = (gt * up * sg * (1.0 + gate * (1.0 - sg))).astype(BF16)
        r.ggu[b, FL:] = (gt * sl).astype(BF16)
        r.gs[b4] = dot(r.ggu[b, :], all_e(), 1, 1).astype(BF16)
        if k == 0:
            send_nm(2)
        if k:
            send(r.gs.at[b4], r.r2.at[y], r.s_r2.at[k], {"seq": s, "ctx": 2 * b4 + xl})
    for k in (0, 1, 3, 2):
        b4 = y if k == 0 else y_from[k]
        r.los[b4] = dot(r.act[rows(b4 * TOK, TOK), :], r.cw[...]).astype(BF16)

    for j in range(4):
        g = dot(r.nm[:, j * 256 : (j + 1) * 256], r.ggu[...], 0, 0).astype(BF16)
        for q in range(4):
            r.ge[q % 2, 2 * j + q // 2] = g[64 * q : 64 * q + 64, :]
    send(r.ge.at[sib], r.ge1, r.s_e1.at[0], me_sib)
    for j in range(2):
        g = dot(r.act[:, j * 384 : (j + 1) * 384], r.dy[...], 0, 0)
        for q in range(16):
            r.gc[q // 8, j, q % 8] = g[24 * q : 24 * q + 24, :].astype(BF16)
    for j in range(2):
        send(r.gc.at[sib, j], r.gc1.at[j], r.s_c4.at[j], me_sib)

    g_mlp = r.gs[y].astype(F32)
    for k in range(1, 4):
        got(r.r2.at[y_peer[k]], r.s_r2.at[k])
        g_mlp = g_mlp + r.r2[y_peer[k]].astype(F32)
    hidden = r.hid[...]
    inv_h = lax.rsqrt(jnp.mean(hidden * hidden, axis=1, keepdims=True) + EPS)
    unit = hidden * inv_h
    feed = jnp.sum(g_mlp * unit, axis=0, keepdims=True)
    g = g_mlp * gain_f
    g = r.dy[my4, :].astype(F32) + inv_h * (g - unit * jnp.mean(g * unit, axis=1, keepdims=True))
    r.gh[...] = g
    r.g4[my4, :] = g.astype(BF16)
    for k in (1, 3, 2):
        send(
            r.g4.at[my4], r.g4.at[my4], r.s_g4.at[k], {"seq": s, "ctx": 2 * y_peer[k] + xl}
        )
    r.gg0[...] = jnp.zeros((24, 128), F32)
    for j in range(8):
        r.gg0[8 + j : 9 + j, :] = feed[:, 128 * j : 128 * j + 128]

    got(r.ge1, r.s_e1.at[0])

    def pair_e(j, _):
        r.ges[j] = (r.ge[core, j].astype(F32) + r.ge1[j].astype(F32)).astype(BF16)
        return 0

    lax.fori_loop(0, 8, pair_e, 0)
    for k in (1, 3, 2):
        send(
            r.ges.at[pl.ds(pl.multiple_of(2 * z_peer[k], 2), 2)], r.ge2.at[z], r.s_e2.at[k],
            at(z_peer[k], xh, core, c),
        )
    for j in range(2):
        got(r.gc1.at[j], r.s_c4.at[j])
        for q in range(8):
            r.gcs[j, q % 2, q // 2] = (
                r.gc[core, j, q].astype(F32) + r.gc1[j, q].astype(F32)
            ).astype(BF16)
    for n, (xx, ll) in enumerate(x_line):
        send(
            r.gcs.at[xx, ll], r.gc2.at[xh * 2 + xl], r.s_c5.at[n],
            at(z, xx, core, 2 * y + ll),
        )

    for k in (0, 1, 3, 2):
        j = y if k == 0 else y_from[k]
        b = rows(j * TOK, TOK)
        if k:
            got(r.g4.at[b], r.s_g4.at[k])
        gm = dot(r.g4[b, :], all_o(), 1, 1).astype(BF16)
        for h in range(4):
            r.gm[h // 2, j, pl.ds((h % 2) * TOK, TOK), :] = gm[:, h * HEAD : (h + 1) * HEAD]

    for k in (1, 3, 2):
        b4 = y_from[k]
        send(r.los.at[b4], r.r3.at[y], r.s_r3.at[k], {"seq": s, "ctx": 2 * b4 + xl})

    for j in range(2):
        g = dot(r.mx[:, j * 256 : (j + 1) * 256], r.g4[...], 0, 0).astype(BF16)
        for q in range(16):
            r.go[q // 8, j, q % 8] = g[16 * q : 16 * q + 16, :]
    for j in range(2):
        send(r.go.at[sib, j], r.go1.at[j], r.s_o4.at[j], me_sib)

    for g in range(2):
        for j in (3, 2, 1, 0):
            n = (2 * j + 2) * TOK
            q, kk, gmh = r.qs[g, j], keys(g, j), r.gm[g, j]
            low = at_p(g, j)[...]
            p = low.astype(F32)
            gat = dot(gmh, keys(2 + g, j), 1, 1)
            ds = (p * (gat - jnp.sum(p * gat, axis=1, keepdims=True))).astype(BF16)
            r.dq[g, j] = dot(ds, kk) * SCALE
            dk = dot(ds, q, 0, 0) * SCALE
            dv = dot(low, gmh, 0, 0)
            kr, vr = g * SEQ, (2 + g) * SEQ
            if j == 3:
                r.f4[kr : kr + n, :] = dk
                r.f4[vr : vr + n, :] = dv
            else:
                r.f4[kr : kr + n, :] += dk
                r.f4[vr : vr + n, :] += dv
            theirs = (2 * j + 1 - xl) * TOK
            r.ds[g, j, 0] = r.f4[rows(kr + theirs, TOK), :].astype(BF16)
            r.ds[g, j, 1] = r.f4[rows(vr + theirs, TOK), :].astype(BF16)
            send(r.ds.at[g, j], r.dr.at[g, j], r.s_dr.at[g, j], x_partner)
            if g or j != 3:
                continue
            for j in range(2):
                got(r.go1.at[j], r.s_o4.at[j])
                for q in range(8):
                    r.gos[j, q % 2, q // 2] = (
                        r.go[core, j, q].astype(F32) + r.go1[j, q].astype(F32)
                    ).astype(BF16)
            for n, (xx, ll) in enumerate(x_line):
                send(
                    r.gos.at[xx, ll], r.go2.at[xh * 2 + xl], r.s_o5.at[n],
                    at(z, xx, core, 2 * y + ll),
                )

    total = r.hid[...] + r.los[y].astype(F32)
    for k in range(1, 4):
        got(r.r3.at[y_peer[k]], r.s_r3.at[k])
        total = total + r.r3[y_peer[k]].astype(F32)
    r.lo[...] = total.astype(BF16)

    r.attg[...] = jnp.zeros((1, D), F32)
    r.hgq[...] = jnp.zeros((1, HEAD), F32)
    r.hgk[...] = jnp.zeros((1, HEAD), F32)

    def norms(g, j):
        b = rows(j * TOK, TOK)
        mine = (2 * j + xl) * TOK
        cosine, sine = r.cos[b, :], r.sin[b, :]
        got(r.dr.at[g, j], r.s_dr.at[g, j])
        for h in (2 * g, 2 * g + 1, 4 + g):
            if h < 4:
                wv = r.dq[g, j, (h % 2) * TOK : (h % 2 + 1) * TOK, :]
            else:
                wv = r.f4[rows(g * SEQ + mine, TOK), :] + r.dr[g, j, 0].astype(F32)
            gn = wv * cosine - turn(wv) * sine
            v = r.pj[b, h * HEAD : (h + 1) * HEAD]
            inv = lax.rsqrt(jnp.mean(v * v, axis=1, keepdims=True) + EPS)
            unit = v * inv
            acc = r.hgq if h < 4 else r.hgk
            acc[...] += jnp.sum(gn * unit, axis=0, keepdims=True)
            t = gn * (gain_q if h < 4 else gain_k)
            gx = inv * (t - unit * jnp.mean(t * unit, axis=1, keepdims=True))
            r.gp[b, HEADS[h] : HEADS[h] + HEAD] = gx.astype(BF16)
        r.gp[b, 640 + g * 256 : 768 + g * 256] = (
            r.f4[rows((2 + g) * SEQ + mine, TOK), :] + r.dr[g, j, 1].astype(F32)
        ).astype(BF16)

    def grad_projection(g):
        half = pl.ds(g * 512, 512)
        for j in range(4):
            left = r.ns[:, j * 256 : (j + 1) * 256]
            for n in range(2):
                t = dot(left, r.gp[:, n * 512 + g * 256 : n * 512 + (g + 1) * 256], 0, 0)
                t = t.astype(BF16)
                at_lane = g * 512 + n * 256
                for q in range(4):
                    first = (q % 2) * 512 + (2 * j + q // 2) * 64
                    r.gpx[first : first + 64, at_lane : at_lane + 256] = t[64 * q : 64 * q + 64, :]
        send(r.gpx.at[rows(sib * 512, 512), half], r.gp1.at[:, half], r.s_p1.at[g], me_sib)

    def pair_projection(g):
        half = pl.ds(g * 512, 512)
        got(r.gp1.at[:, half], r.s_p1.at[g])
        r.gpx[D:, half] = (
            r.gpx[rows(core * 512, 512), half].astype(F32) + r.gp1[:, half].astype(F32)
        ).astype(BF16)
        for k in range(1, 8):
            send(
                r.gpx.at[rows(D + w_peer[k] * 64, 64), half], r.gp2.at[w, :, half],
                r.s_p2.at[g, k], on_w(w_peer[k], core, c),
            )

    for j in (3, 2, 1, 0):
        norms(0, j)
    grad_projection(0)
    for j in (3, 2, 1, 0):
        norms(1, j)
    grad_projection(1)
    pair_projection(0)
    for k in (1, 3, 2):
        got(r.ge2.at[z_from[k]], r.s_e2.at[k])
    for xx in range(2):
        total = r.ges[2 * z + xx].astype(F32)
        for k in range(1, 4):
            total = total + r.ge2[z_from[k], xx].astype(F32)
        r.get[xx] = total.astype(BF16)
    send(r.get.at[1 - xh], r.gex, r.s_ex.at[0], at(z, 1 - xh, core, c))

    for k in (2, 1, 3, 0):
        j = y_peer[k] if k else y
        b = rows(j * TOK, TOK)
        part = dot(r.gp[b, :], all_p(0, D), 1, 1)
        r.ps[j] = part.astype(BF16)
        if k:
            send(r.ps.at[j], r.r1.at[y], r.s_r4.at[y], {"seq": s, "ctx": 2 * j + xl})
        v = r.xs[b, :].astype(F32)
        inv = lax.rsqrt(jnp.mean(v * v, axis=1, keepdims=True) + EPS)
        r.attg[...] += jnp.sum(part * (v * inv), axis=0, keepdims=True)

    for j in range(8):
        r.gg0[j : j + 1, :] = r.attg[:, 128 * j : 128 * j + 128]
    r.gg0[16:17, :] = r.hgq[...]
    r.gg0[17:18, :] = r.hgk[...]
    send(r.gg0, r.gg1, r.s_a1.at[0], me_sib)

    got(r.gg1, r.s_a1.at[0])
    r.ggt[...] = r.gg0[...] + r.gg1[...]
    for k in range(1, 8):
        send(r.ggt, r.gg2.at[w], r.s_a2.at[k], on_w(w_peer[k], core, c))

    pair_projection(1)

    got(r.gex, r.s_ex.at[0])
    total = r.get[xh].astype(F32) + r.gex[...].astype(F32)
    for j in range(8):
        r.gef[j] = total[8 * j : 8 * j + 8, :].astype(BF16)
    for k in range(1, 8):
        send(r.gef.at[ctx_peer[k]], r.ge3.at[c], r.s_e3.at[k], {"seq": s, "ctx": ctx_peer[k]})
    r.ge3[c] = r.gef[c]
    for n, (xx, ll) in enumerate(x_line):
        got(r.gc2.at[xx * 2 + ll], r.s_c5.at[n])
    for n, (xx, ll) in enumerate(x_line):
        got(r.go2.at[xx * 2 + ll], r.s_o5.at[n])
    for mine, theirs, out, last, sem in (
        (r.gcs, r.gc2, r.gcf, r.gc3, r.s_c6), (r.gos, r.go2, r.gof, r.go3, r.s_o6),
    ):
        for j in range(4):
            total = mine[xh, xl, j].astype(F32)
            for xx, ll in x_line:
                total = total + theirs[xx * 2 + ll, j].astype(F32)
            out[j] = total.astype(BF16)
            send(
                out.at[j], last.at[z], sem.at[z], at(y, xh, core, 2 * j + xl),
                unless=diag & (y == j),
            )

    @pl.when(diag)
    def _():
        r.gc3[z] = r.gcf[y]
        r.go3[z] = r.gof[y]

    total = r.ggt[...]
    for k in range(1, 8):
        got(r.gg2.at[w_from[k]], r.s_a2.at[k])
        total = total + r.gg2[w_from[k]]
    r.ggt2[...] = total
    for k in range(1, 8):
        send(r.ggt2, r.gg3.at[c], r.s_a3.at[k], {"seq": s, "ctx": ctx_peer[k]})

    for g in range(2):
        for k in range(1, 8):
            got(r.gp2.at[w_from[k], :, pl.ds(g * 512, 512)], r.s_p2.at[g, k])
    total = r.gpx[rows(D + w * 64, 64), :].astype(F32)
    for k in range(1, 8):
        total = total + r.gp2[w_from[k]].astype(F32)
    for j in range(8):
        r.gpf[j] = total[8 * j : 8 * j + 8, :].astype(BF16)
    for k in range(1, 8):
        send(r.gpf.at[ctx_peer[k]], r.gp3.at[c], r.s_p3.at[k], {"seq": s, "ctx": ctx_peer[k]})
    r.gp3[c] = r.gpf[c]

    for k in range(1, 8):
        got(r.ge3.at[ctx_from[k]], r.s_e3.at[k])
    for j in range(4):
        t = r.ge3[2 * j].astype(F32) + r.ge3[2 * j + 1].astype(F32)
        r.geo[:, j * FL : (j + 1) * FL] = t[:, :FL]
        r.geo[:, FF + j * FL : FF + (j + 1) * FL] = t[:, FL:]
    for j in range(4):

        @pl.when(jnp.logical_not(diag & (z == j)))
        def _():
            got(r.gc3.at[j], r.s_c6.at[j])
            got(r.go3.at[j], r.s_o6.at[j])

    for last, out in ((r.gc3, r.gco), (r.go3, r.goo)):
        out[...] = (last[0].astype(F32) + last[1].astype(F32)) + (
            last[2].astype(F32) + last[3].astype(F32)
        )

    total = r.gh[...]
    g = r.ps[y].astype(F32)
    for k in range(1, 4):
        got(r.r1.at[y_from[k]], r.s_r4.at[y_from[k]])
        g = g + r.r1[y_from[k]].astype(F32)
    v = r.xs[my4, :].astype(F32)
    inv = lax.rsqrt(jnp.mean(v * v, axis=1, keepdims=True) + EPS)
    unit = v * inv
    g = g * gain_a
    r.gt[...] = total + inv * (g - unit * jnp.mean(g * unit, axis=1, keepdims=True))

    for k in range(1, 8):
        got(r.gp3.at[ctx_from[k]], r.s_p3.at[k])
    for j in range(4):
        t = r.gp3[2 * j].astype(F32) + r.gp3[2 * j + 1].astype(F32)
        for place, (start, size) in PLACES:
            n = 0 if start < 512 else 1 if start < 768 else 2
            to = PCOLS[n][0] + j * PCOLS[n][1] + start - PCOLS[n][2]
            r.gpo[:, to : to + size] = t[:, place : place + size]
    total = r.ggt2[...]
    for k in range(1, 8):
        got(r.gg3.at[ctx_from[k]], r.s_a3.at[k])
        total = total + r.gg3[ctx_from[k]]
    r.ggo[...] = total

    finish(list(sends))


def hand_over(ggo, lo, gt, gpo, goo, geo, gco, *refs):
    outs, (ag, fg, hg), kept, sem = refs[:6], refs[6:9], refs[9:15], refs[15]
    ins = (lo, gt, gpo, goo, geo, gco)
    loads = [pltpu.make_async_copy(ins[n], kept[n], sem.at[n]) for n in range(6)]
    stores = [pltpu.make_async_copy(kept[n], outs[n], sem.at[6 + n]) for n in range(6)]
    for cp in loads:
        cp.start()
    for load, store in zip(loads, stores, strict=True):
        load.wait()
        store.start()
    place = 8 * lax.axis_index("seq") + lax.axis_index("ctx")
    row = lax.broadcasted_iota(jnp.int32, (8, 128), 0)
    lane = lax.broadcasted_iota(jnp.int32, (8, 128), 1)
    for n, (ref, size) in enumerate(((ag, 8), (fg, 8), (hg, 2))):
        tile = ggo[8 * n : 8 * n + 8, :]
        got = jnp.zeros((1, size), F32)
        at = lax.broadcasted_iota(jnp.int32, (1, size), 1)
        for j in range(size):
            value = jnp.where(row * 128 + lane == place * size + j, tile, 0.0)
            value = jnp.sum(jnp.sum(value, axis=1, keepdims=True), axis=0, keepdims=True)
            got = jnp.where(at == j, value, got)
        ref[...] = got
    for cp in stores:
        cp.wait()


def per_device(x, dy, segments, positions, ag, proj, hg, out, fg, expn, con):
    del positions
    vmem = pl.BlockSpec(memory_space=pltpu.VMEM)
    hbm = pl.BlockSpec(memory_space=pl.ANY)
    scratch = [pltpu.VMEM(shape, kind) for shape, kind in SCRATCH.values()]
    sems = [pltpu.SemaphoreType.DMA(n if isinstance(n, tuple) else (n,)) for n in RECV.values()]
    res = pl.pallas_call(
        kernel,
        name="layer",
        out_shape=(
            jax.ShapeDtypeStruct((TOK, D), BF16),
            jax.ShapeDtypeStruct((TOK, D), F32),
            jax.ShapeDtypeStruct((8, 4096), F32),
            jax.ShapeDtypeStruct((16, D), F32),
            jax.ShapeDtypeStruct((8, 6144), F32),
            jax.ShapeDtypeStruct((24, D), F32),
            jax.ShapeDtypeStruct((24, 128), F32),
        ),
        in_specs=[hbm] * 6 + [vmem] * 4,
        out_specs=(vmem,) * 7,
        scratch_shapes=scratch
        + sems
        + [pltpu.SemaphoreType.DMA((N_SEND,)), pltpu.SemaphoreType.DMA((16,))],
        compiler_params=pltpu.CompilerParams(
            collective_id=0, has_side_effects=True, vmem_limit_bytes=63 * 2**20
        ),
    )(
        x.reshape(TOK, D), dy.reshape(TOK, D), proj, out, expn, con,
        ag.reshape(1, 8), fg.reshape(1, 8), hg.reshape(1, 2), segments,
    )
    big, gains = res[:6], res[6]
    lo, gt, gpo, goo, geo, gco, gag, gfg, ghg = pl.pallas_call(
        hand_over,
        name="hand_over",
        out_shape=tuple(jax.ShapeDtypeStruct(a.shape, a.dtype) for a in big)
        + tuple(jax.ShapeDtypeStruct((1, n), F32) for n in (8, 8, 2)),
        in_specs=[vmem] + [pl.BlockSpec(memory_space=pltpu.HBM)] * 6,
        out_specs=(pl.BlockSpec(memory_space=pltpu.HBM),) * 6 + (vmem,) * 3,
        scratch_shapes=[pltpu.VMEM(a.shape, a.dtype) for a in big]
        + [pltpu.SemaphoreType.DMA((12,))],
        compiler_params=pltpu.CompilerParams(vmem_limit_bytes=63 * 2**20),
    )(gains, *big)
    return (
        lo.reshape(1, TOK, D),
        gt.reshape(1, TOK, D),
        gag.reshape(8),
        gpo,
        ghg.reshape(2),
        goo,
        gfg.reshape(8),
        geo,
        gco,
    )


def solution(mesh):
    return jax.shard_map(
        per_device,
        mesh=mesh,
        in_specs=(
            P("seq", "ctx", None),
            P("seq", "ctx", None),
            P("seq", None),
            P("seq", "ctx"),
            P(("seq", "ctx")),
            P(("seq", "ctx"), None),
            P(("seq", "ctx")),
            P(("seq", "ctx"), None),
            P(("seq", "ctx")),
            P(("seq", "ctx"), None),
            P(("seq", "ctx"), None),
        ),
        out_specs=(
            P("seq", "ctx", None),
            P("seq", "ctx", None),
            P(("seq", "ctx")),
            P(("seq", "ctx"), None),
            P(("seq", "ctx")),
            P(("seq", "ctx"), None),
            P(("seq", "ctx")),
            P(("seq", "ctx"), None),
            P(("seq", "ctx"), None),
        ),
        check_vma=False,
    )
```

profile of v0, /device:TPU:4, one launch (start us, length us, event | category | flops | bytes accessed | tf_op | source)
XLA Modules:
  0.0 160.8 jit_solution(14571633284960112044)
XLA Ops:
  0.6 156.5 %layer.1 = (bf16[128,1024]{1,0:T(8,128)(2,1)}, f32[128,1024]{1,0:T(8,128)}, f32[8,4096]{1,0:T(8,128)}, f32[16,1024]{1,0:T(8,128)}, f32[8,6144]{1,0:T(8,128)}, /*index=5*/f32[24,1024]{1,0:T(8,128)}, f32[24,128]{1,0:T(8,128)}) custom-call(bf16[128,1024]{1,0:T(8,128)(2,1)} %bitcast.10, bf16[128,1024]{1,0:T(8,128)(2,1)} %bitcast.11, bf16[8,4096]{1,0:T(8,128)(2,1)} %refs_2_.1, ...), custom_call_target="tpu_custom_call" | custom-call | tf_op jit(solution)/shard_map/layer/pallas_call | solution.py:911
  157.2 3.4 %hand_over.1 = (bf16[128,1024]{1,0:T(8,128)(2,1)}, f32[128,1024]{1,0:T(8,128)}, f32[8,4096]{1,0:T(8,128)}, f32[16,1024]{1,0:T(8,128)}, f32[8,6144]{1,0:T(8,128)}...) custom-call(f32[24,128]{1,0:T(8,128)} %get-tuple-element.25.ggo, ...), custom_call_target="tpu_custom_call" | custom-call | tf_op jit(solution)/shard_map/hand_over/pallas_call | solution.py:936
where the time goes:
time: 161 us
  Pallas kernels  160 us (99%)
    pallas_call x1, Pallas kernels, per_device(): pl.pallas_call(kernel, name='layer', out_shape=(jax.ShapeDtypeStruct((TOK...  157 us
    pallas_call x1, Pallas kernels, per_device(): pl.pallas_call(hand_over, name='hand_over', out_shape=tuple((jax.ShapeDty...  3.4 us

commit v1 on v0

--- a/solution.py
+++ b/solution.py
@@ -114,7 +114,7 @@
     o1=4, o2=4, o3=2, c1=4, c2=4, c3=2, kv=4, r1=4, nm=4, r2=4, r3=4, g4=4, dr=(2, 4), r4=4,
     e1=1, e2=4, ex=1, e3=8, c4=2, c5=4, c6=4, o4=2, o5=4, o6=4, p1=2, p2=(2, 8), p3=8, a1=1, a2=8, a3=8,
 )
-N_SEND = 160
+N_SEND = 88
 NAMES = (
     ["x", "dyi", "pi", "oi", "ei", "ci", "agi", "fgi", "hgi", "segr"]
     + ["lo", "gt", "gpo", "goo", "geo", "gco", "ggo"]
@@ -267,7 +267,7 @@
                 r.s_pa.at[k, min(part, 1)],
                 {"seq": s, "ctx": to},
             )
-    for k in (1, 3, 2):
+    for k in (1, 3):
         send(r.x, r.xs.at[my4], r.s_x.at[k], {"seq": s, "ctx": 2 * y_peer[k] + xl})
 
     @pl.when(diag)
@@ -337,7 +337,9 @@
     for g in range(2):
         r.pw[w, core, :, 512 + g * 256 : 640 + g * 256] = joined(512 + g * 128, 128)
         r.pw[w, core, :, 640 + g * 256 : 768 + g * 256] = joined(768 + g * 128, 128)
+    first_sends = list(sends)
     spread(0, kv_half)
+    send(r.x, r.xs.at[my4], r.s_x.at[2], {"seq": s, "ctx": 2 * y_peer[2] + xl})
     for k in range(1, 8):
         to = ctx_peer[k]
         for part in range(2):
@@ -428,6 +430,8 @@
         for h in range(4):
             u = headed(out[:, h * HEAD : (h + 1) * HEAD], b, h)
             r.qs[h // 2, j, pl.ds((h % 2) * TOK, TOK), :] = u
+    finish(first_sends)
+
     for j in range(4):
 
         @pl.when(jnp.logical_not(diag & (y == j)))
@@ -595,10 +599,13 @@
     g = r.dy[my4, :].astype(F32) + inv_h * (g - unit * jnp.mean(g * unit, axis=1, keepdims=True))
     r.gh[...] = g
     r.g4[my4, :] = g.astype(BF16)
-    for k in (1, 3, 2):
+    def send_g4(k):
         send(
             r.g4.at[my4], r.g4.at[my4], r.s_g4.at[k], {"seq": s, "ctx": 2 * y_peer[k] + xl}
         )
+
+    send_g4(1)
+    send_g4(3)
     r.gg0[...] = jnp.zeros((24, 128), F32)
     for j in range(8):
         r.gg0[8 + j : 9 + j, :] = feed[:, 128 * j : 128 * j + 128]
@@ -627,6 +634,8 @@
             at(z, xx, core, 2 * y + ll),
         )
 
+    send_g4(2)
+
     for k in (0, 1, 3, 2):
         j = y if k == 0 else y_from[k]
         b = rows(j * TOK, TOK)
@@ -636,6 +645,7 @@
         for h in range(4):
             r.gm[h // 2, j, pl.ds((h % 2) * TOK, TOK), :] = gm[:, h * HEAD : (h + 1) * HEAD]
 
+    older = list(sends)
     for k in (1, 3, 2):
         b4 = y_from[k]
         send(r.los.at[b4], r.r3.at[y], r.s_r3.at[k], {"seq": s, "ctx": 2 * b4 + xl})
@@ -741,6 +751,7 @@
                 r.s_p2.at[g, k], on_w(w_peer[k], core, c),
             )
 
+    finish(older)
     for j in (3, 2, 1, 0):
         norms(0, j)
     grad_projection(0)

time: 161 us -> 160 us (level)
  no operation moved by 1% of the time
where the time goes in v1:
time: 160 us
  Pallas kernels  159 us (99%)
    pallas_call x1, Pallas kernels, per_device(): pl.pallas_call(kernel, name='layer', out_shape=(jax.ShapeDtypeStruct((TOK...  156 us
    pallas_call x1, Pallas kernels, per_device(): pl.pallas_call(hand_over, name='hand_over', out_shape=tuple((jax.ShapeDty...  3.4 us

profile of v1, /device:TPU:4, one launch (start us, length us, event | category | flops | bytes accessed | tf_op | source)
XLA Modules:
  0.0 160.1 jit_solution(7571551931915205583)
XLA Ops:
  0.6 155.8 %layer.1 = (bf16[128,1024]{1,0:T(8,128)(2,1)}, f32[128,1024]{1,0:T(8,128)}, f32[8,4096]{1,0:T(8,128)}, f32[16,1024]{1,0:T(8,128)}, f32[8,6144]{1,0:T(8,128)}, /*index=5*/f32[24,1024]{1,0:T(8,128)}, f32[24,128]{1,0:T(8,128)}) custom-call(bf16[128,1024]{1,0:T(8,128)(2,1)} %bitcast.10, bf16[128,1024]{1,0:T(8,128)(2,1)} %bitcast.11, bf16[8,4096]{1,0:T(8,128)(2,1)} %refs_2_.1, ...), custom_call_target="tpu_custom_call" | custom-call | tf_op jit(solution)/shard_map/layer/pallas_call | solution.py:922
  156.5 3.4 %hand_over.1 = (bf16[128,1024]{1,0:T(8,128)(2,1)}, f32[128,1024]{1,0:T(8,128)}, f32[8,4096]{1,0:T(8,128)}, f32[16,1024]{1,0:T(8,128)}, f32[8,6144]{1,0:T(8,128)}...) custom-call(f32[24,128]{1,0:T(8,128)} %get-tuple-element.25.ggo, ...), custom_call_target="tpu_custom_call" | custom-call | tf_op jit(solution)/shard_map/hand_over/pallas_call | solution.py:947

commit v2 on v1

--- a/solution.py
+++ b/solution.py
@@ -755,10 +755,7 @@
     for j in (3, 2, 1, 0):
         norms(0, j)
     grad_projection(0)
-    for j in (3, 2, 1, 0):
-        norms(1, j)
-    grad_projection(1)
-    pair_projection(0)
+
     for k in (1, 3, 2):
         got(r.ge2.at[z_from[k]], r.s_e2.at[k])
     for xx in range(2):
@@ -768,6 +765,11 @@
         r.get[xx] = total.astype(BF16)
     send(r.get.at[1 - xh], r.gex, r.s_ex.at[0], at(z, 1 - xh, core, c))
 
+    pair_projection(0)
+
+    for j in (3, 2, 1, 0):
+        norms(1, j)
+    grad_projection(1)
     for k in (2, 1, 3, 0):
         j = y_peer[k] if k else y
         b = rows(j * TOK, TOK)

time: 160 us -> 159 us (level); the launches traced: 160 us -> 157 us
  Pallas kernels: 159 us -> 156 us
    pallas_call x1, Pallas kernels: 156 us -> 152 us  [per_device(): pl.pallas_call(kernel, name='layer', out_shape=(jax.ShapeDtypeStruct((TOK...]
where the time goes in v2:
time: 159 us; the launch traced here: 157 us
  Pallas kernels  156 us (98%)
    pallas_call x1, Pallas kernels, per_device(): pl.pallas_call(kernel, name='layer', out_shape=(jax.ShapeDtypeStruct((TOK...  152 us
    pallas_call x1, Pallas kernels, per_device(): pl.pallas_call(hand_over, name='hand_over', out_shape=tuple((jax.ShapeDty...  3.4 us

profile of v2, /device:TPU:4, one launch (start us, length us, event | category | flops | bytes accessed | tf_op | source)
XLA Modules:
  0.0 156.6 jit_solution(13661172455671031657)
XLA Ops:
  0.6 152.4 %layer.1 = (bf16[128,1024]{1,0:T(8,128)(2,1)}, f32[128,1024]{1,0:T(8,128)}, f32[8,4096]{1,0:T(8,128)}, f32[16,1024]{1,0:T(8,128)}, f32[8,6144]{1,0:T(8,128)}, /*index=5*/f32[24,1024]{1,0:T(8,128)}, f32[24,128]{1,0:T(8,128)}) custom-call(bf16[128,1024]{1,0:T(8,128)(2,1)} %bitcast.10, bf16[128,1024]{1,0:T(8,128)(2,1)} %bitcast.11, bf16[8,4096]{1,0:T(8,128)(2,1)} %refs_2_.1, ...), custom_call_target="tpu_custom_call" | custom-call | tf_op jit(solution)/shard_map/layer/pallas_call | solution.py:924
  153.0 3.4 %hand_over.1 = (bf16[128,1024]{1,0:T(8,128)(2,1)}, f32[128,1024]{1,0:T(8,128)}, f32[8,4096]{1,0:T(8,128)}, f32[16,1024]{1,0:T(8,128)}, f32[8,6144]{1,0:T(8,128)}...) custom-call(f32[24,128]{1,0:T(8,128)} %get-tuple-element.25.ggo, ...), custom_call_target="tpu_custom_call" | custom-call | tf_op jit(solution)/shard_map/hand_over/pallas_call | solution.py:949
